TPU v7x, 32 devices: a whole 2x2x4 slice. The times are simulated.
32 devices in a mesh: space: 16 (over z, y, x), sens: 2 (over core).
Axes of the slice: x: 2, y: 2, z: 4, core: 2. Of those that a mesh axis runs over, the one named last changes fastest.
Arguments:
- adjoint_end: float32 [16, 64, 64, 128], P('sens', 'space'), may hold values from -6 to 6
- checkpoints: float32 [8, 64, 64, 128], P('sens', 'space'), may hold values from 0.5 to 2
- dispersion: float32 [6, 64, 64, 128], P(None, 'space', 'sens'), as said below
- owner_steps: int32 [3], replicated, may hold values from 0 to 7, as said below
- sensor_cells: int32 [16], P('sens'), may hold values from 0 to 524287
- misfit: float32 [16, 3], P('sens'), may hold values from -6 to 6
- release_cells: int32 [128], replicated, may hold values from 0 to 524287
- release_steps: int32 [128], replicated, may hold values from 0 to 2
Outputs:
- adjoint: float32 [16, 64, 64, 128], P('sens', 'space')
- release_grad: float32 [16, 128], P('sens')
Inputs may be any that keep to these rules, and one draw needn't show every extreme that they name: `owner_steps`: the entries are different stored states; the first and the last stored state are always among them. `sensor_cells`: flat cell indices. `release_cells`: flat cell indices. `dispersion`: zz, yy and xx components are positive.
All inputs are finite; a program needn't handle non-finite values.
Results may differ from a plain program's by a relative error of at most 0.00002.
Values sent between devices are 32-bit elements; how exact they have to be, the bound alone decides.
No kernel may reach another device: no remote copies, remote signals or barrier semaphores. Data moves between devices by JAX's collectives and lax.ppermute only.
A program may use at most 128 MiB of HBM per device.

v0:
```python
import jax
import jax.numpy as jnp
from jax import lax
from jax.sharding import PartitionSpec as P

STEPS = 3
step_dt = 0.12


def extended(block, sides, width):
    for axis, dim in sides:
        count = lax.axis_size(axis)
        forward = [(i, i + 1) for i in range(count - 1)]
        backward = [(target, source) for source, target in forward]
        low = lax.ppermute(
            lax.slice_in_dim(block, block.shape[dim] - width, None, axis=dim), axis, forward
        )
        high = lax.ppermute(lax.slice_in_dim(block, 0, width, axis=dim), axis, backward)
        block = jnp.concatenate([low, block, high], axis=dim)
    return block


def broadcast(array, axis, root):
    mine = lax.axis_index(axis) == root
    return lax.psum(jnp.where(mine, array, jnp.zeros_like(array)), axis)


def retard_scale(conc):
    return step_dt / (1.0 + 0.5 * conc ** (-0.5))


def retard_slope(conc):
    retard = 1.0 + 0.5 * conc ** (-0.5)
    deriv = -0.25 * conc ** (-1.5)
    return -step_dt * deriv / (retard * retard)


def apply_op(field, tensor):
    depth = field.shape[1] - 2
    rows_y = field.shape[2]
    rows_x = field.shape[3]
    padded = jnp.pad(field, ((0, 0), (0, 0), (1, 1), (1, 1)))
    coeffs = jnp.pad(tensor, ((0, 0), (0, 0), (1, 1), (1, 1)))

    def at_shift(arr, shift):
        return arr[
            ...,
            1 + shift[0] : 1 + shift[0] + depth,
            1 + shift[1] : 1 + shift[1] + rows_y,
            1 + shift[2] : 1 + shift[2] + rows_x,
        ]

    units = [(1, 0, 0), (0, 1, 0), (0, 0, 1)]
    centre = (0, 0, 0)
    total = jnp.zeros((field.shape[0], depth, rows_y, rows_x), jnp.float32)
    for axis_id in range(3):
        plus = units[axis_id]
        minus = tuple((-v for v in plus))
        diag = coeffs[axis_id]
        a_plus = 0.5 * (at_shift(diag, centre) + at_shift(diag, plus))
        a_minus = 0.5 * (at_shift(diag, centre) + at_shift(diag, minus))
        total = total + a_plus * (at_shift(padded, plus) - at_shift(padded, centre))
        total = total - a_minus * (at_shift(padded, centre) - at_shift(padded, minus))
    for first, second, comp in ((0, 1, 3), (0, 2, 4), (1, 2, 5)):
        for outer, inner in ((first, second), (second, first)):
            unit_o = units[outer]
            unit_i = units[inner]
            for sign in (1, -1):
                spot = tuple((sign * v for v in unit_o))
                up_spot = tuple((spot[t] + unit_i[t] for t in range(3)))
                down_spot = tuple((spot[t] - unit_i[t] for t in range(3)))
                flux = at_shift(coeffs[comp], spot) * (
                    0.5 * (at_shift(padded, up_spot) - at_shift(padded, down_spot))
                )
                total = total + 0.5 * sign * flux
    return total


def add_misfit(field, column, sensor_cells, start_cell):
    count = field.shape[0]
    cells = field.shape[1] * field.shape[2] * field.shape[3]
    local = sensor_cells - start_cell
    positions = lax.broadcasted_iota(jnp.int32, (count, cells), 1)
    hit = positions == local[:, None]
    return field + jnp.where(hit, column[:, None], 0.0).reshape(field.shape)


def body(
    adjoint_end,
    checkpoints,
    dispersion,
    owner_steps,
    sensor_cells,
    misfit,
    release_cells,
    release_steps,
):
    own_sensors, depth, rows_y, rows_x = adjoint_end.shape
    slot_count = checkpoints.shape[0]
    cells = depth * rows_y * rows_x
    first_cell = lax.axis_index("space") * cells
    release_local = release_cells - first_cell
    release_inside = (release_local >= 0) & (release_local < cells)
    release_index = jnp.clip(release_local, 0, cells - 1)
    lam = adjoint_end
    partial_grad = jnp.zeros((own_sensors, release_cells.shape[0]), jnp.float32)
    whole = lax.all_gather(dispersion, "sens", axis=2, tiled=True)
    tensor = extended(whole, (("space", 1),), 1)
    for step in reversed(range(STEPS)):
        holder = owner_steps[step] // slot_count
        mine = lax.dynamic_index_in_dim(
            checkpoints, owner_steps[step] % slot_count, 0, keepdims=False
        )
        conc = broadcast(mine, "sens", holder)
        mixed = add_misfit(lam, misfit[:, step], sensor_cells, first_cell)
        scaled = retard_scale(conc) * mixed
        stacked = jnp.concatenate([conc[None], scaled], 0)
        rimmed = extended(stacked, (("space", 1),), 1)
        applied = apply_op(rimmed, tensor)
        lam = mixed + applied[1:] + retard_slope(conc) * applied[0] * mixed
        values = jnp.take(lam.reshape(own_sensors, cells), release_index, axis=1)
        keep = release_inside & (release_steps == step)
        partial_grad = partial_grad + jnp.where(keep[None, :], values, 0.0)
    release_grad = lax.psum(partial_grad, "space")
    return (lam, release_grad)


def solution(mesh):
    in_specs = (
        P("sens", "space", None, None),
        P("sens", "space", None, None),
        P(None, "space", "sens", None),
        P(),
        P("sens"),
        P("sens", None),
        P(),
        P(),
    )
    out_specs = (P("sens", "space", None, None), P("sens", None))
    return jax.shard_map(body, mesh=mesh, in_specs=in_specs, out_specs=out_specs, check_vma=False)
```

profile of v0, /device:TPU:0, one launch (start us, length us, event | category | flops | bytes accessed | tf_op | source)
XLA Modules:
  0.0 248.9 jit_solution(358271755512530131)
XLA Ops:
  7.2 0.0 all-reduce.7.cloned.1.call-start
  7.2 2.8 %all_gather.3 = f32[6,4,64,128]{3,2,1,0:T(8,128)S(1)} all-gather(f32[6,4,32,128]{3,2,1,0:T(8,128)} %param.12), channel_id=1, replica_groups=mesh['space'=16,'sens'=2] {'sens'}, dimensions={2}, use_global_device_ids=true | all-gather | bytes 1179648 | tf_op jit(solution)/shard_map/all_gather | solution.py:107
  10.1 4.8 %collective-permute-start = (f32[6,1,64,128]{3,2,1,0:T(8,128)S(1)}, f32[6,1,64,128]{3,2,1,0:T(8,128)S(1)}, u32[]{:S(2)}, u32[]{:S(2)}) collective-permute-start(f32[6,1,64,128]{3,2,1,0:T(8,128)S(1)} %get-tuple-element.28), channel_id=1, source_target_pairs={{0,2},{2,4},{4,6},{6,8},{8,10},{10,12},{12,14},{14,16},{16,18},{18... | collective-permute-start | bytes 589832 | tf_op jit(solution)/shard_map/ppermute | solution.py:15
  14.8 1.3 collective-permute-start.1
  16.2 0.6 fusion.113
  24.6 0.8 select_bitcast_fusion
  25.3 0.0 all-reduce.7.cloned.1.call-update
  25.4 0.0 copy-done.58
  25.4 0.0 collective-permute-done
  25.4 0.0 collective-permute-done.1
  25.5 0.8 select_maximum_fusion.9
  26.2 1.2 slice_bitcast_fusion.5
  27.4 1.0 slice_multiply_fusion.11
  28.5 0.3 slice_multiply_fusion.3
  28.8 17.7 %all-reduce.7.cloned.1.call-done = (f32[4,64,128]{2,1,0:T(8,128)}, f32[4,64,128]{2,1,0:T(8,128)}, f32[4,64,128]{2,1,0:T(8,128)}) async-done(((f32[4,64,128]{2,1,0:T(8,128)}, f32[4,64,128]{2,1,0:T(8,128)}, f32[4,64,128]{2,1,0:T(8,128)}), (f32[4,64,128]{2,1,0:T(8,128)}, f32[4,64,128]{2,1,0:T(8,128)}, f32[4,64,128]{2,1,0:T(8,128)})) %all-reduce.7.cloned.1.call-update) | async-done | bytes 393232 | tf_op jit(solution)/shard_map/psum | solution.py:25
  46.5 1.0 fusion.107
  47.5 0.3 fusion.89
  47.8 0.0 copy-start.48
  47.8 0.6 copy-done.4
  48.4 3.7 %collective-permute-start.3 = (f32[9,1,64,128]{3,2,1,0:T(8,128)S(1)}, f32[9,1,64,128]{3,2,1,0:T(8,128)S(1)}, u32[]{:S(2)}, u32[]{:S(2)}) collective-permute-start(f32[9,1,64,128]{3,2,1,0:T(8,128)S(1)} %get-tuple-element.26), channel_id=1, source_target_pairs={{0,2},{2,4},{4,6},{6,8},{8,10},{10,12},{12,14},{14,16},{16,18},{18... | collective-permute-start | bytes 884744 | tf_op jit(solution)/shard_map/ppermute | solution.py:15
  52.1 1.3 collective-permute-start.2
  53.4 0.0 copy-done.48
  53.4 0.0 copy-done.49
  53.5 0.3 fusion.102
  53.8 0.1 fusion.106
  53.9 11.3 %collective-permute-done.3 = f32[9,1,64,128]{3,2,1,0:T(8,128)S(1)} collective-permute-done((f32[9,1,64,128]{3,2,1,0:T(8,128)S(1)}, f32[9,1,64,128]{3,2,1,0:T(8,128)S(1)}, u32[]{:S(2)}, u32[]{:S(2)}) %collective-permute-start.3) | collective-permute-done | bytes 294944 | tf_op jit(solution)/shard_map/ppermute | solution.py:15
  65.1 1.9 collective-permute-done.2
  67.1 2.7 %select_maximum_fusion.6 = f32[9,6,66,130]{3,2,1,0:T(8,128)S(1)} fusion(f32[9,1,64,128]{3,2,1,0:T(8,128)S(1)} %collective-permute-done.2, f32[9,1,64,128]{3,2,1,0:T(8,128)S(1)} %collective-permute-done.3, f32[8,4,64,128]{3,2,1,0:T(8,128)S(1)} %fusion.89, f32[1,4,64,128]{3,2,1,0:T(8,128)S(1)} %bitcast.69), kind=kLoop, calls=%fused_computation.13 | loop fusion | flops 8339760 | bytes 3622752 | tf_op jit(solution)/shard_map/concatenate | solution.py:19
  69.9 4.7 %fusion.69 = f32[9,4,64,128]{3,2,1,0:T(8,128)S(1)} fusion(f32[9,6,66,130]{3,2,1,0:T(8,128)S(1)} %select_maximum_fusion.6, f32[9,1,64,128]{3,2,1,0:T(8,128)S(1)} %collective-permute-done.3, f32[8,4,64,128]{3,2,1,0:T(8,128)S(1)} %fusion.89, f32[1,4,64,128]{3,2,1,0:T(8,128)S(1)} %bitcast.70, f32[9,1,64,128]{3,2,1,0:T(8,128)S(1)} %collective-permute-done.2, ...), kind=kLoop, calls=%fused_computation.120 | loop fusion | flops 20643840 | bytes 24182784 | tf_op jit(solution)/shard_map/add | solution.py:75
  74.5 0.1 fusion.98
  74.6 0.6 fusion.88
  75.2 0.0 copy-start.57
  75.2 0.0 copy-start.59
  75.3 3.4 %collective-permute-start.5 = (f32[9,1,64,128]{3,2,1,0:T(8,128)S(1)}, f32[9,1,64,128]{3,2,1,0:T(8,128)S(1)}, u32[]{:S(2)}, u32[]{:S(2)}) collective-permute-start(f32[9,1,64,128]{3,2,1,0:T(8,128)S(1)} %get-tuple-element.24), channel_id=1, source_target_pairs={{0,2},{2,4},{4,6},{6,8},{8,10},{10,12},{12,14},{14,16},{16,18},{18... | collective-permute-start | bytes 884744 | tf_op jit(solution)/shard_map/ppermute | solution.py:15
  78.7 1.5 collective-permute-start.4
  80.2 0.6 compare_and_fusion.3
  80.8 0.1 fusion.105
  80.9 10.0 %collective-permute-done.5 = f32[9,1,64,128]{3,2,1,0:T(8,128)S(1)} collective-permute-done((f32[9,1,64,128]{3,2,1,0:T(8,128)S(1)}, f32[9,1,64,128]{3,2,1,0:T(8,128)S(1)}, u32[]{:S(2)}, u32[]{:S(2)}) %collective-permute-start.5) | collective-permute-done | bytes 294944 | tf_op jit(solution)/shard_map/ppermute | solution.py:15
  90.9 0.7 collective-permute-done.4
  91.6 2.7 %select_maximum_fusion.3 = f32[9,6,66,130]{3,2,1,0:T(8,128)S(1)} fusion(f32[9,1,64,128]{3,2,1,0:T(8,128)S(1)} %collective-permute-done.4, f32[9,1,64,128]{3,2,1,0:T(8,128)S(1)} %collective-permute-done.5, f32[8,4,64,128]{3,2,1,0:T(8,128)S(1)} %get-tuple-element.14, f32[1,4,64,128]{3,2,1,0:T(8,128)S(1)} %bitcast.66), kind=kLoop, calls=%fused_computation.10 | loop fusion | flops 8339760 | bytes 3622752 | tf_op jit(solution)/shard_map/concatenate | solution.py:19
  94.4 4.7 %fusion.44 = f32[9,4,64,128]{3,2,1,0:T(8,128)S(1)} fusion(f32[9,6,66,130]{3,2,1,0:T(8,128)S(1)} %select_maximum_fusion.3, f32[9,1,64,128]{3,2,1,0:T(8,128)S(1)} %collective-permute-done.5, f32[8,4,64,128]{3,2,1,0:T(8,128)S(1)} %get-tuple-element.14, f32[1,4,64,128]{3,2,1,0:T(8,128)S(1)} %bitcast.67, f32[9,1,64,128]{3,2,1,0:T(8,128)S(1)} %collective-permute-done.4, ...), kind=kLoop, calls=%fused_computation.87 | loop fusion | flops 20643840 | bytes 24182784 | tf_op jit(solution)/shard_map/add | solution.py:75
  99.1 0.1 fusion.97
  99.2 0.6 fusion.87
  99.8 0.8 fusion.91
  100.6 4.3 %collective-permute-start.7 = (f32[9,1,64,128]{3,2,1,0:T(8,128)}, f32[9,1,64,128]{3,2,1,0:T(8,128)}, u32[]{:S(2)}, u32[]{:S(2)}) collective-permute-start(f32[9,1,64,128]{3,2,1,0:T(8,128)} %get-tuple-element.22), channel_id=1, source_target_pairs={{0,2},{2,4},{4,6},{6,8},{8,10},{10,12},{12,14},{14,16},{16,18},{18... | collective-permute-start | bytes 884744 | tf_op jit(solution)/shard_map/ppermute | solution.py:15
  105.0 1.3 collective-permute-start.6
  106.3 0.5 compare_and_fusion.2
  106.8 8.7 %copy.10 = f32[8,4,64,128]{0,3,2,1:T(8,128)} copy(f32[8,4,64,128]{3,2,1,0:T(8,128)S(1)} %get-tuple-element.15) | data formatting | bytes 2097152 | tf_op jit(solution)/shard_map/add | solution.py:120
  115.5 7.0 %gather_fusion = f32[128,8]{1,0:T(8,128)} fusion(f32[8,32768]{0,1:T(8,128)} %bitcast.59, s32[1024]{0:T(1024)S(1)} %pad_clamp_fusion), kind=kCustom, calls=%fused_computation.clone | custom fusion | bytes 8704 | tf_op jit(solution)/shard_map/jit(_take)/gather | solution.py:121
  122.5 8.7 %copy.11 = f32[8,4,64,128]{0,3,2,1:T(8,128)} copy(f32[8,4,64,128]{3,2,1,0:T(8,128)S(1)} %get-tuple-element.13) | data formatting | bytes 2097152 | tf_op jit(solution)/shard_map/add | solution.py:120
  131.1 7.0 %gather_fusion.1 = f32[128,8]{1,0:T(8,128)} fusion(f32[8,32768]{0,1:T(8,128)} %bitcast.61, s32[1024]{0:T(1024)S(1)} %pad_clamp_fusion), kind=kCustom, calls=%fused_computation.1.clone | custom fusion | bytes 8704 | tf_op jit(solution)/shard_map/jit(_take)/gather | solution.py:121
  138.3 0.0 collective-permute-done.7
  138.3 0.0 collective-permute-done.6
  138.3 3.9 %select_maximum_fusion = f32[9,6,66,130]{3,2,1,0:T(8,128)S(1)} fusion(f32[9,1,64,128]{3,2,1,0:T(8,128)} %collective-permute-done.6, f32[9,1,64,128]{3,2,1,0:T(8,128)} %collective-permute-done.7, f32[8,4,64,128]{3,2,1,0:T(8,128)S(1)} %get-tuple-element.12, f32[1,4,64,128]{3,2,1,0:T(8,128)S(1)} %bitcast.63), kind=kLoop, calls=%fused_computation.7 | loop fusion | flops 8339760 | bytes 3622752 | tf_op jit(solution)/shard_map/concatenate | solution.py:19
  142.4 5.7 %fusion.19 = f32[9,4,64,128]{3,2,1,0:T(8,128)S(1)} fusion(f32[9,6,66,130]{3,2,1,0:T(8,128)S(1)} %select_maximum_fusion, f32[9,1,64,128]{3,2,1,0:T(8,128)} %collective-permute-done.7, f32[8,4,64,128]{3,2,1,0:T(8,128)S(1)} %get-tuple-element.12, f32[1,4,64,128]{3,2,1,0:T(8,128)S(1)} %bitcast.64, f32[9,1,64,128]{3,2,1,0:T(8,128)} %collective-permute-done.6, ...), kind=kLoop, calls=%fused_computation.54 | loop fusion | flops 20643840 | bytes 24182784 | tf_op jit(solution)/shard_map/add | solution.py:75
  148.1 0.1 fusion.96
  148.2 0.4 fusion.84
  148.6 0.0 copy-start
  148.6 0.0 copy-start.54
  148.6 8.7 %copy.12 = f32[8,4,64,128]{0,3,2,1:T(8,128)} copy(f32[8,4,64,128]{3,2,1,0:T(8,128)S(1)} %fusion.84) | data formatting | bytes 2097152 | tf_op jit(solution)/shard_map/add | solution.py:120
  157.4 6.4 %gather_fusion.2 = f32[128,8]{1,0:T(8,128)S(1)} fusion(f32[8,32768]{0,1:T(8,128)} %bitcast.60, s32[1024]{0:T(1024)S(1)} %pad_clamp_fusion), kind=kCustom, calls=%fused_computation.2.clone | custom fusion | bytes 8704 | tf_op jit(solution)/shard_map/jit(_take)/gather | solution.py:121
  163.8 0.1 fusion.108
  164.0 77.5 %psum.31 = f32[8,128]{0,1:T(8,128)S(1)} all-reduce(f32[8,128]{0,1:T(8,128)S(1)} %fusion.108), channel_id=1, replica_groups=mesh['space'=16,'sens'=2] {'space'}, use_global_device_ids=true, to_apply=%region_3.5 | all-reduce | flops 1024 | bytes 8192 | tf_op jit(solution)/shard_map/psum | solution.py:124
  241.4 0.7 copy.13
  (120 shorter events, 0.4 us)
Async XLA Ops:
  7.2 9.0 %copy-start.53 = (s32[3]{0:T(128)S(1)}, s32[3]{0:T(128)}, u32[]{:S(2)}) copy-start(s32[3]{0:T(128)} %param.13) | copy-start | bytes 40
  7.2 17.4 %copy-start.50 = (f32[4,4,64,128]{3,2,1,0:T(8,128)S(1)}, f32[4,4,64,128]{3,2,1,0:T(8,128)}, u32[]{:S(2)}) copy-start(f32[4,4,64,128]{3,2,1,0:T(8,128)} %param.11) | copy-start | bytes 1572868
  7.2 39.3 %all-reduce.7.cloned.1.call-start = ((), (), s32[]{:S(2)}) async-start(), calls=%async_computation | async-start | bytes 786432 | tf_op jit(solution)/shard_map/psum | solution.py:25
  10.0 15.4 %copy-start.58 = (f32[8,3]{0,1:T(4,128)S(1)}, f32[8,3]{0,1:T(4,128)}, u32[]{:S(2)}) copy-start(f32[8,3]{0,1:T(4,128)} %param.15) | copy-start | bytes 292
  10.0 15.4 %copy-start.60 = (s32[8]{0:T(128)S(1)}, s32[8]{0:T(128)}, u32[]{:S(2)}) copy-start(s32[8]{0:T(128)} %param.14) | copy-start | bytes 100
  10.1 15.4 %collective-permute-start = (f32[6,1,64,128]{3,2,1,0:T(8,128)S(1)}, f32[6,1,64,128]{3,2,1,0:T(8,128)S(1)}, u32[]{:S(2)}, u32[]{:S(2)}) collective-permute-start(f32[6,1,64,128]{3,2,1,0:T(8,128)S(1)} %get-tuple-element.28), channel_id=1, source_target_pairs={{0,2},{2,4},{4,6},{6,8},{8,10},{10,12},{12,14},{14,16},{16,18},{18... | collective-permute-start | bytes 589832 | tf_op jit(solution)/shard_map/ppermute | solution.py:15
  14.8 10.6 %collective-permute-start.1 = (f32[6,1,64,128]{3,2,1,0:T(8,128)S(1)}, f32[6,1,64,128]{3,2,1,0:T(8,128)S(1)}, u32[]{:S(2)}, u32[]{:S(2)}) collective-permute-start(f32[6,1,64,128]{3,2,1,0:T(8,128)S(1)} %get-tuple-element.29), channel_id=1, source_target_pairs={{2,0},{4,2},{6,4},{8,6},{10,8},{12,10},{14,12},{16,14},{18,16},{20... | collective-permute-start | bytes 589832 | tf_op jit(solution)/shard_map/ppermute | solution.py:18
  28.4 41.3 %copy-start.33 = (f32[4,64,128]{2,1,0:T(8,128)}, f32[4,64,128]{2,1,0:T(8,128)S(1)}, u32[]{:S(2)}) copy-start(f32[4,64,128]{2,1,0:T(8,128)S(1)} %get-tuple-element.39) | copy-start | bytes 393220
  28.5 41.3 %copy-start.36 = (f32[4,64,128]{2,1,0:T(8,128)}, f32[4,64,128]{2,1,0:T(8,128)S(1)}, u32[]{:S(2)}) copy-start(f32[4,64,128]{2,1,0:T(8,128)S(1)} %get-tuple-element.40) | copy-start | bytes 393220
  28.5 41.3 %copy-start.39 = (f32[4,64,128]{2,1,0:T(8,128)}, f32[4,64,128]{2,1,0:T(8,128)S(1)}, u32[]{:S(2)}) copy-start(f32[4,64,128]{2,1,0:T(8,128)S(1)} %get-tuple-element.41) | copy-start | bytes 393220
  28.5 19.0 %copy-start.1 = (f32[8,4,64,128]{3,2,1,0:T(8,128)S(1)}, f32[8,4,64,128]{3,2,1,0:T(8,128)}, u32[]{:S(2)}) copy-start(f32[8,4,64,128]{3,2,1,0:T(8,128)} %param.10) | copy-start | bytes 3145732
  28.7 41.0 %copy-start.7 = (f32[4,64,128]{2,1,0:T(8,128)}, f32[4,64,128]{2,1,0:T(8,128)S(1)}, u32[]{:S(2)}) copy-start(f32[4,64,128]{2,1,0:T(8,128)S(1)} %get-tuple-element.49) | copy-start | bytes 393220
  28.8 41.0 %copy-start.10 = (f32[4,64,128]{2,1,0:T(8,128)}, f32[4,64,128]{2,1,0:T(8,128)S(1)}, u32[]{:S(2)}) copy-start(f32[4,64,128]{2,1,0:T(8,128)S(1)} %get-tuple-element.50) | copy-start | bytes 393220
  28.8 41.0 %copy-start.13 = (f32[4,64,128]{2,1,0:T(8,128)}, f32[4,64,128]{2,1,0:T(8,128)S(1)}, u32[]{:S(2)}) copy-start(f32[4,64,128]{2,1,0:T(8,128)S(1)} %get-tuple-element.61) | copy-start | bytes 393220
  28.8 41.0 %copy-start.16 = (f32[4,64,128]{2,1,0:T(8,128)}, f32[4,64,128]{2,1,0:T(8,128)S(1)}, u32[]{:S(2)}) copy-start(f32[4,64,128]{2,1,0:T(8,128)S(1)} %get-tuple-element.62) | copy-start | bytes 393220
  28.8 41.0 %copy-start.19 = (f32[4,64,128]{2,1,0:T(8,128)}, f32[4,64,128]{2,1,0:T(8,128)S(1)}, u32[]{:S(2)}) copy-start(f32[4,64,128]{2,1,0:T(8,128)S(1)} %get-tuple-element.63) | copy-start | bytes 393220
  28.8 41.0 %copy-start.22 = (f32[4,64,128]{2,1,0:T(8,128)}, f32[4,64,128]{2,1,0:T(8,128)S(1)}, u32[]{:S(2)}) copy-start(f32[4,64,128]{2,1,0:T(8,128)S(1)} %get-tuple-element.64) | copy-start | bytes 393220
  28.8 65.5 %copy-start.5 = (f32[4,64,128]{2,1,0:T(8,128)}, f32[4,64,128]{2,1,0:T(8,128)S(1)}, u32[]{:S(2)}) copy-start(f32[4,64,128]{2,1,0:T(8,128)S(1)} %get-tuple-element.48) | copy-start | bytes 393220
  47.8 5.7 %copy-start.48 = (f32[6,66,130]{2,1,0:T(8,128)S(1)}, f32[6,66,130]{2,1,0:T(8,128)}, u32[]{:S(2)}) copy-start(f32[6,66,130]{2,1,0:T(8,128)} %get-tuple-element.16) | copy-start | bytes 617764
  47.8 5.7 %copy-start.49 = (f32[6,66,130]{2,1,0:T(8,128)S(1)}, f32[6,66,130]{2,1,0:T(8,128)}, u32[]{:S(2)}) copy-start(f32[6,66,130]{2,1,0:T(8,128)} %get-tuple-element.20) | copy-start | bytes 617764
  48.4 5.4 %copy-start.3 = (f32[4,64,128]{2,1,0:T(8,128)S(1)}, f32[4,64,128]{2,1,0:T(8,128)}, u32[]{:S(2)}) copy-start(f32[4,64,128]{2,1,0:T(8,128)} %get-tuple-element.6) | copy-start | bytes 393220
  48.4 16.7 %collective-permute-start.3 = (f32[9,1,64,128]{3,2,1,0:T(8,128)S(1)}, f32[9,1,64,128]{3,2,1,0:T(8,128)S(1)}, u32[]{:S(2)}, u32[]{:S(2)}) collective-permute-start(f32[9,1,64,128]{3,2,1,0:T(8,128)S(1)} %get-tuple-element.26), channel_id=1, source_target_pairs={{0,2},{2,4},{4,6},{6,8},{8,10},{10,12},{12,14},{14,16},{16,18},{18... | collective-permute-start | bytes 884744 | tf_op jit(solution)/shard_map/ppermute | solution.py:15
  52.1 14.9 %collective-permute-start.2 = (f32[9,1,64,128]{3,2,1,0:T(8,128)S(1)}, f32[9,1,64,128]{3,2,1,0:T(8,128)S(1)}, u32[]{:S(2)}, u32[]{:S(2)}) collective-permute-start(f32[9,1,64,128]{3,2,1,0:T(8,128)S(1)} %get-tuple-element.27), channel_id=1, source_target_pairs={{2,0},{4,2},{6,4},{8,6},{10,8},{12,10},{14,12},{16,14},{18,16},{20... | collective-permute-start | bytes 884744 | tf_op jit(solution)/shard_map/ppermute | solution.py:18
  53.7 40.6 %copy-start.25 = (f32[4,64,128]{2,1,0:T(8,128)}, f32[4,64,128]{2,1,0:T(8,128)S(1)}, u32[]{:S(2)}) copy-start(f32[4,64,128]{2,1,0:T(8,128)S(1)} %get-tuple-element.35) | copy-start | bytes 393220
  53.7 40.6 %copy-start.27 = (f32[4,64,128]{2,1,0:T(8,128)}, f32[4,64,128]{2,1,0:T(8,128)S(1)}, u32[]{:S(2)}) copy-start(f32[4,64,128]{2,1,0:T(8,128)S(1)} %get-tuple-element.36) | copy-start | bytes 393220
  53.8 40.6 %copy-start.29 = (f32[4,64,128]{2,1,0:T(8,128)}, f32[4,64,128]{2,1,0:T(8,128)S(1)}, u32[]{:S(2)}) copy-start(f32[4,64,128]{2,1,0:T(8,128)S(1)} %get-tuple-element.67) | copy-start | bytes 393220
  53.8 40.6 %copy-start.31 = (f32[4,64,128]{2,1,0:T(8,128)}, f32[4,64,128]{2,1,0:T(8,128)S(1)}, u32[]{:S(2)}) copy-start(f32[4,64,128]{2,1,0:T(8,128)S(1)} %get-tuple-element.68) | copy-start | bytes 393220
  53.9 16.0 %copy-start.42 = (f32[4,64,128]{2,1,0:T(8,128)S(1)}, f32[4,64,128]{2,1,0:T(8,128)}, u32[]{:S(2)}) copy-start(f32[4,64,128]{2,1,0:T(8,128)} %get-tuple-element.42) | copy-start | bytes 393220
  53.9 16.0 %copy-start.44 = (f32[4,64,128]{2,1,0:T(8,128)S(1)}, f32[4,64,128]{2,1,0:T(8,128)}, u32[]{:S(2)}) copy-start(f32[4,64,128]{2,1,0:T(8,128)} %get-tuple-element.65) | copy-start | bytes 393220
  53.9 16.0 %copy-start.46 = (f32[4,64,128]{2,1,0:T(8,128)S(1)}, f32[4,64,128]{2,1,0:T(8,128)}, u32[]{:S(2)}) copy-start(f32[4,64,128]{2,1,0:T(8,128)} %get-tuple-element.66) | copy-start | bytes 393220
  75.2 5.0 %copy-start.57 = (s32[128]{0:T(128)S(1)}, s32[128]{0:T(128)}, u32[]{:S(2)}) copy-start(s32[128]{0:T(128)} %param.17) | copy-start | bytes 1540
  75.2 5.0 %copy-start.59 = (s32[128]{0:T(128)S(1)}, s32[128]{0:T(128)}, u32[]{:S(2)}) copy-start(s32[128]{0:T(128)} %param.16) | copy-start | bytes 1540
  75.2 5.5 %copy-start.2 = (f32[4,64,128]{2,1,0:T(8,128)S(1)}, f32[4,64,128]{2,1,0:T(8,128)}, u32[]{:S(2)}) copy-start(f32[4,64,128]{2,1,0:T(8,128)} %get-tuple-element.7) | copy-start | bytes 393220
  75.3 15.6 %collective-permute-start.5 = (f32[9,1,64,128]{3,2,1,0:T(8,128)S(1)}, f32[9,1,64,128]{3,2,1,0:T(8,128)S(1)}, u32[]{:S(2)}, u32[]{:S(2)}) collective-permute-start(f32[9,1,64,128]{3,2,1,0:T(8,128)S(1)} %get-tuple-element.24), channel_id=1, source_target_pairs={{0,2},{2,4},{4,6},{6,8},{8,10},{10,12},{12,14},{14,16},{16,18},{18... | collective-permute-start | bytes 884744 | tf_op jit(solution)/shard_map/ppermute | solution.py:15
  78.7 12.9 %collective-permute-start.4 = (f32[9,1,64,128]{3,2,1,0:T(8,128)S(1)}, f32[9,1,64,128]{3,2,1,0:T(8,128)S(1)}, u32[]{:S(2)}, u32[]{:S(2)}) collective-permute-start(f32[9,1,64,128]{3,2,1,0:T(8,128)S(1)} %get-tuple-element.25), channel_id=1, source_target_pairs={{2,0},{4,2},{6,4},{8,6},{10,8},{12,10},{14,12},{16,14},{18,16},{20... | collective-permute-start | bytes 884744 | tf_op jit(solution)/shard_map/ppermute | solution.py:18
  80.8 13.5 %copy-start.8 = (f32[4,64,128]{2,1,0:T(8,128)S(1)}, f32[4,64,128]{2,1,0:T(8,128)}, u32[]{:S(2)}) copy-start(f32[4,64,128]{2,1,0:T(8,128)} %copy-done.7) | copy-start | bytes 393220
  80.8 13.5 %copy-start.11 = (f32[4,64,128]{2,1,0:T(8,128)S(1)}, f32[4,64,128]{2,1,0:T(8,128)}, u32[]{:S(2)}) copy-start(f32[4,64,128]{2,1,0:T(8,128)} %copy-done.10) | copy-start | bytes 393220
  80.9 13.5 %copy-start.14 = (f32[4,64,128]{2,1,0:T(8,128)S(1)}, f32[4,64,128]{2,1,0:T(8,128)}, u32[]{:S(2)}) copy-start(f32[4,64,128]{2,1,0:T(8,128)} %copy-done.13) | copy-start | bytes 393220
  80.9 13.5 %copy-start.17 = (f32[4,64,128]{2,1,0:T(8,128)S(1)}, f32[4,64,128]{2,1,0:T(8,128)}, u32[]{:S(2)}) copy-start(f32[4,64,128]{2,1,0:T(8,128)} %copy-done.16) | copy-start | bytes 393220
  80.9 13.5 %copy-start.20 = (f32[4,64,128]{2,1,0:T(8,128)S(1)}, f32[4,64,128]{2,1,0:T(8,128)}, u32[]{:S(2)}) copy-start(f32[4,64,128]{2,1,0:T(8,128)} %copy-done.19) | copy-start | bytes 393220
  80.9 13.5 %copy-start.23 = (f32[4,64,128]{2,1,0:T(8,128)S(1)}, f32[4,64,128]{2,1,0:T(8,128)}, u32[]{:S(2)}) copy-start(f32[4,64,128]{2,1,0:T(8,128)} %copy-done.22) | copy-start | bytes 393220
  80.9 13.5 %copy-start.34 = (f32[4,64,128]{2,1,0:T(8,128)S(1)}, f32[4,64,128]{2,1,0:T(8,128)}, u32[]{:S(2)}) copy-start(f32[4,64,128]{2,1,0:T(8,128)} %copy-done.33) | copy-start | bytes 393220
  80.9 13.5 %copy-start.37 = (f32[4,64,128]{2,1,0:T(8,128)S(1)}, f32[4,64,128]{2,1,0:T(8,128)}, u32[]{:S(2)}) copy-start(f32[4,64,128]{2,1,0:T(8,128)} %copy-done.36) | copy-start | bytes 393220
  80.9 13.5 %copy-start.40 = (f32[4,64,128]{2,1,0:T(8,128)S(1)}, f32[4,64,128]{2,1,0:T(8,128)}, u32[]{:S(2)}) copy-start(f32[4,64,128]{2,1,0:T(8,128)} %copy-done.39) | copy-start | bytes 393220
  100.6 37.6 %collective-permute-start.7 = (f32[9,1,64,128]{3,2,1,0:T(8,128)}, f32[9,1,64,128]{3,2,1,0:T(8,128)}, u32[]{:S(2)}, u32[]{:S(2)}) collective-permute-start(f32[9,1,64,128]{3,2,1,0:T(8,128)} %get-tuple-element.22), channel_id=1, source_target_pairs={{0,2},{2,4},{4,6},{6,8},{8,10},{10,12},{12,14},{14,16},{16,18},{18... | collective-permute-start | bytes 884744 | tf_op jit(solution)/shard_map/ppermute | solution.py:15
  105.0 33.3 %collective-permute-start.6 = (f32[9,1,64,128]{3,2,1,0:T(8,128)}, f32[9,1,64,128]{3,2,1,0:T(8,128)}, u32[]{:S(2)}, u32[]{:S(2)}) collective-permute-start(f32[9,1,64,128]{3,2,1,0:T(8,128)} %get-tuple-element.23), channel_id=1, source_target_pairs={{2,0},{4,2},{6,4},{8,6},{10,8},{12,10},{14,12},{16,14},{18,16},{20... | collective-permute-start | bytes 884744 | tf_op jit(solution)/shard_map/ppermute | solution.py:18
  138.1 4.1 %copy-start.18 = (f32[4,64,128]{2,1,0:T(8,128)S(1)}, f32[4,64,128]{2,1,0:T(8,128)}, u32[]{:S(2)}) copy-start(f32[4,64,128]{2,1,0:T(8,128)} %copy-done.16) | copy-start | bytes 393220
  138.1 4.1 %copy-start.21 = (f32[4,64,128]{2,1,0:T(8,128)S(1)}, f32[4,64,128]{2,1,0:T(8,128)}, u32[]{:S(2)}) copy-start(f32[4,64,128]{2,1,0:T(8,128)} %copy-done.19) | copy-start | bytes 393220
  138.1 4.1 %copy-start.24 = (f32[4,64,128]{2,1,0:T(8,128)S(1)}, f32[4,64,128]{2,1,0:T(8,128)}, u32[]{:S(2)}) copy-start(f32[4,64,128]{2,1,0:T(8,128)} %copy-done.22) | copy-start | bytes 393220
  138.2 4.1 %copy-start.26 = (f32[4,64,128]{2,1,0:T(8,128)S(1)}, f32[4,64,128]{2,1,0:T(8,128)}, u32[]{:S(2)}) copy-start(f32[4,64,128]{2,1,0:T(8,128)} %copy-done.25) | copy-start | bytes 393220
  138.2 4.1 %copy-start.28 = (f32[4,64,128]{2,1,0:T(8,128)S(1)}, f32[4,64,128]{2,1,0:T(8,128)}, u32[]{:S(2)}) copy-start(f32[4,64,128]{2,1,0:T(8,128)} %copy-done.27) | copy-start | bytes 393220
  138.2 4.1 %copy-start.30 = (f32[4,64,128]{2,1,0:T(8,128)S(1)}, f32[4,64,128]{2,1,0:T(8,128)}, u32[]{:S(2)}) copy-start(f32[4,64,128]{2,1,0:T(8,128)} %copy-done.29) | copy-start | bytes 393220
  138.2 4.1 %copy-start.32 = (f32[4,64,128]{2,1,0:T(8,128)S(1)}, f32[4,64,128]{2,1,0:T(8,128)}, u32[]{:S(2)}) copy-start(f32[4,64,128]{2,1,0:T(8,128)} %copy-done.31) | copy-start | bytes 393220
  138.2 4.1 %copy-start.35 = (f32[4,64,128]{2,1,0:T(8,128)S(1)}, f32[4,64,128]{2,1,0:T(8,128)}, u32[]{:S(2)}) copy-start(f32[4,64,128]{2,1,0:T(8,128)} %copy-done.33) | copy-start | bytes 393220
  138.2 4.1 %copy-start.38 = (f32[4,64,128]{2,1,0:T(8,128)S(1)}, f32[4,64,128]{2,1,0:T(8,128)}, u32[]{:S(2)}) copy-start(f32[4,64,128]{2,1,0:T(8,128)} %copy-done.36) | copy-start | bytes 393220
  138.2 4.1 %copy-start.41 = (f32[4,64,128]{2,1,0:T(8,128)S(1)}, f32[4,64,128]{2,1,0:T(8,128)}, u32[]{:S(2)}) copy-start(f32[4,64,128]{2,1,0:T(8,128)} %copy-done.39) | copy-start | bytes 393220
  138.2 4.1 %copy-start.43 = (f32[4,64,128]{2,1,0:T(8,128)S(1)}, f32[4,64,128]{2,1,0:T(8,128)}, u32[]{:S(2)}) copy-start(f32[4,64,128]{2,1,0:T(8,128)} %get-tuple-element.42) | copy-start | bytes 393220
  138.2 4.1 %copy-start.45 = (f32[4,64,128]{2,1,0:T(8,128)S(1)}, f32[4,64,128]{2,1,0:T(8,128)}, u32[]{:S(2)}) copy-start(f32[4,64,128]{2,1,0:T(8,128)} %get-tuple-element.65) | copy-start | bytes 393220
  148.6 8.8 %copy-start = (f32[8,4,64,128]{3,2,1,0:T(8,128)}, f32[8,4,64,128]{3,2,1,0:T(8,128)S(1)}, u32[]{:S(2)}) copy-start(f32[8,4,64,128]{3,2,1,0:T(8,128)S(1)} %fusion.84) | copy-start | bytes 3145732
  148.6 15.2 %copy-start.51 = (f32[128,8]{1,0:T(8,128)S(1)}, f32[128,8]{1,0:T(8,128)}, u32[]{:S(2)}) copy-start(f32[128,8]{1,0:T(8,128)} %gather_fusion) | copy-start | bytes 12292
  148.6 15.2 %copy-start.52 = (f32[128,8]{1,0:T(8,128)S(1)}, f32[128,8]{1,0:T(8,128)}, u32[]{:S(2)}) copy-start(f32[128,8]{1,0:T(8,128)} %gather_fusion.1) | copy-start | bytes 12292
  148.6 15.2 %copy-start.54 = (pred[128]{0:T(512)(128)(4,1)S(1)}, pred[128]{0:T(512)(128)(4,1)}, u32[]{:S(2)}) copy-start(pred[128]{0:T(512)(128)(4,1)} %get-tuple-element.8) | copy-start | bytes 388
  148.6 15.2 %copy-start.55 = (pred[128]{0:T(512)(128)(4,1)S(1)}, pred[128]{0:T(512)(128)(4,1)}, u32[]{:S(2)}) copy-start(pred[128]{0:T(512)(128)(4,1)} %get-tuple-element.56) | copy-start | bytes 388
  148.6 15.2 %copy-start.56 = (pred[128]{0:T(512)(128)(4,1)S(1)}, pred[128]{0:T(512)(128)(4,1)}, u32[]{:S(2)}) copy-start(pred[128]{0:T(512)(128)(4,1)} %get-tuple-element.55) | copy-start | bytes 388
  (6 other events, 21.4 us)
Sparse Core Ops, SparseCore 0:
  25.5 20.9 all-reduce.6
where the time goes:
time: 250 us; the launch traced here: 249 us
  blocking collectives  80.2 us (32%)
  local copies, waits for them, and re-layouts  49.8 us (20%)
  waiting for transfers between devices  41.6 us (17%)
  other arithmetic  32.7 us (13%)
  between operations  23 us (9%)
  starting transfers between devices  21.6 us (9%)
    psum x1, blocking collectives, body(): release_grad = lax.psum(partial_grad, 'space')  77.5 us
    add x3, local copies, waits for them, and re-layouts, body(): lam = mixed + applied[1:] + retard_slope(conc) * applied[0] * mixed  26 us
    ppermute x4, waiting for transfers between devices, extended(): lax.ppermute(lax.slice_in_dim(block, block.shape[dim] - width, None, axis...  21.2 us
    gather x3, local copies, waits for them, and re-layouts, body(): values = jnp.take(lam.reshape(own_sensors, cells), release_index, axis=1)  20.4 us
    psum x1, waiting for transfers between devices, broadcast(): return lax.psum(jnp.where(mine, array, jnp.zeros_like(array)), axis)  17.7 us
    ppermute x4, starting transfers between devices, extended(): lax.ppermute(lax.slice_in_dim(block, block.shape[dim] - width, None, axis...  16.2 us
    add x3, other arithmetic, apply_op(): total = total + 0.5 * sign * flux  15 us
    concatenate x4, other arithmetic, extended(): block = jnp.concatenate([low, block, high], axis=dim)  9.99 us
  transfers between devices with their start and end apart: 9, of which 5 were waited for; matrix products, arithmetic and copies ran while one was open for 15% of the time, Pallas kernels for 0%

commit v1 on v0

--- a/solution.py
+++ b/solution.py
@@ -121,7 +121,11 @@
         values = jnp.take(lam.reshape(own_sensors, cells), release_index, axis=1)
         keep = release_inside & (release_steps == step)
         partial_grad = partial_grad + jnp.where(keep[None, :], values, 0.0)
-    release_grad = lax.psum(partial_grad, "space")
+    release_grad = partial_grad
+    for hop in (1, 2, 4, 8):
+        release_grad = release_grad + lax.ppermute(
+            release_grad, "space", [(dev, dev ^ hop) for dev in range(16)]
+        )
     return (lam, release_grad)
 
 

time: 250 us -> 195 us (0.78)
  blocking collectives: 80.2 us -> 2.79 us
  starting transfers between devices: 21.6 us -> 32.9 us
  waiting for transfers between devices: 41.6 us -> 52.5 us
    psum x1 -> x0, blocking collectives: 77.5 us -> none  [body(): release_grad = lax.psum(partial_grad, 'space')]
    ppermute x0 -> x4, starting transfers between devices: none -> 11.3 us  [body(): lax.ppermute(release_grad, 'space', [(dev, dev ^ hop) for dev in range(16)])]
    ppermute x0 -> x4, waiting for transfers between devices: none -> 10.7 us  [body(): lax.ppermute(release_grad, 'space', [(dev, dev ^ hop) for dev in range(16)])]
  transfers between devices with their start and end apart: 9 -> 13, of which waited for: 5 -> 9; matrix products, arithmetic and copies ran while one was open for 15% -> 19% of each run, Pallas kernels for 0% -> 0%
where the time goes in v1:
time: 195 us; the launch traced here: 194 us
  waiting for transfers between devices  52.5 us (27%)
  local copies, waits for them, and re-layouts  50 us (26%)
  starting transfers between devices  32.9 us (17%)
  other arithmetic  32.7 us (17%)
  between operations  22.9 us (12%)
  blocking collectives  2.79 us (1%)
    add x3, local copies, waits for them, and re-layouts, body(): lam = mixed + applied[1:] + retard_slope(conc) * applied[0] * mixed  26.2 us
    ppermute x4, waiting for transfers between devices, extended(): lax.ppermute(lax.slice_in_dim(block, block.shape[dim] - width, None, axis...  21.3 us
    gather x3, local copies, waits for them, and re-layouts, body(): values = jnp.take(lam.reshape(own_sensors, cells), release_index, axis=1)  20.4 us
    psum x1, waiting for transfers between devices, broadcast(): return lax.psum(jnp.where(mine, array, jnp.zeros_like(array)), axis)  17.7 us
    ppermute x4, starting transfers between devices, extended(): lax.ppermute(lax.slice_in_dim(block, block.shape[dim] - width, None, axis...  16.2 us
    add x3, other arithmetic, apply_op(): total = total + 0.5 * sign * flux  15 us
    ppermute x4, starting transfers between devices, body(): lax.ppermute(release_grad, 'space', [(dev, dev ^ hop) for dev in range(16)])  11.3 us
    ppermute x4, waiting for transfers between devices, body(): lax.ppermute(release_grad, 'space', [(dev, dev ^ hop) for dev in range(16)])  10.7 us
  transfers between devices with their start and end apart: 13, of which 9 were waited for; matrix products, arithmetic and copies ran while one was open for 19% of the time, Pallas kernels for 0%

profile of v1, /device:TPU:0, one launch (start us, length us, event | category | flops | bytes accessed | tf_op | source)
XLA Modules:
  0.0 193.9 jit_solution(5476605386013216134)
XLA Ops:
  7.2 0.0 all-reduce.7.cloned.1.call-start
  7.2 2.8 %all_gather.3 = f32[6,4,64,128]{3,2,1,0:T(8,128)S(1)} all-gather(f32[6,4,32,128]{3,2,1,0:T(8,128)} %param.12), channel_id=1, replica_groups=mesh['space'=16,'sens'=2] {'sens'}, dimensions={2}, use_global_device_ids=true | all-gather | bytes 1179648 | tf_op jit(solution)/shard_map/all_gather | solution.py:107
  10.1 4.8 %collective-permute-start = (f32[6,1,64,128]{3,2,1,0:T(8,128)S(1)}, f32[6,1,64,128]{3,2,1,0:T(8,128)S(1)}, u32[]{:S(2)}, u32[]{:S(2)}) collective-permute-start(f32[6,1,64,128]{3,2,1,0:T(8,128)S(1)} %get-tuple-element.28), channel_id=1, source_target_pairs={{0,2},{2,4},{4,6},{6,8},{8,10},{10,12},{12,14},{14,16},{16,18},{18... | collective-permute-start | bytes 589832 | tf_op jit(solution)/shard_map/ppermute | solution.py:15
  14.8 1.3 collective-permute-start.1
  16.2 0.6 fusion.113
  24.5 0.8 select_bitcast_fusion
  25.3 0.0 all-reduce.7.cloned.1.call-update
  25.4 0.8 select_maximum_fusion.9
  26.2 1.2 slice_bitcast_fusion.5
  27.4 1.0 slice_multiply_fusion.11
  28.4 0.3 slice_multiply_fusion.3
  28.7 17.7 %all-reduce.7.cloned.1.call-done = (f32[4,64,128]{2,1,0:T(8,128)}, f32[4,64,128]{2,1,0:T(8,128)}, f32[4,64,128]{2,1,0:T(8,128)}) async-done(((f32[4,64,128]{2,1,0:T(8,128)}, f32[4,64,128]{2,1,0:T(8,128)}, f32[4,64,128]{2,1,0:T(8,128)}), (f32[4,64,128]{2,1,0:T(8,128)}, f32[4,64,128]{2,1,0:T(8,128)}, f32[4,64,128]{2,1,0:T(8,128)})) %all-reduce.7.cloned.1.call-update) | async-done | bytes 393232 | tf_op jit(solution)/shard_map/psum | solution.py:25
  46.5 1.0 fusion.107
  47.5 0.3 fusion.89
  47.7 0.0 copy-start.48
  47.8 0.6 copy-done.4
  48.4 3.7 %collective-permute-start.3 = (f32[9,1,64,128]{3,2,1,0:T(8,128)S(1)}, f32[9,1,64,128]{3,2,1,0:T(8,128)S(1)}, u32[]{:S(2)}, u32[]{:S(2)}) collective-permute-start(f32[9,1,64,128]{3,2,1,0:T(8,128)S(1)} %get-tuple-element.26), channel_id=1, source_target_pairs={{0,2},{2,4},{4,6},{6,8},{8,10},{10,12},{12,14},{14,16},{16,18},{18... | collective-permute-start | bytes 884744 | tf_op jit(solution)/shard_map/ppermute | solution.py:15
  52.1 1.3 collective-permute-start.2
  53.4 0.3 fusion.102
  53.8 0.1 fusion.106
  53.9 11.3 %collective-permute-done.3 = f32[9,1,64,128]{3,2,1,0:T(8,128)S(1)} collective-permute-done((f32[9,1,64,128]{3,2,1,0:T(8,128)S(1)}, f32[9,1,64,128]{3,2,1,0:T(8,128)S(1)}, u32[]{:S(2)}, u32[]{:S(2)}) %collective-permute-start.3) | collective-permute-done | bytes 294944 | tf_op jit(solution)/shard_map/ppermute | solution.py:15
  65.1 1.9 collective-permute-done.2
  67.0 2.7 %select_maximum_fusion.6 = f32[9,6,66,130]{3,2,1,0:T(8,128)S(1)} fusion(f32[9,1,64,128]{3,2,1,0:T(8,128)S(1)} %collective-permute-done.2, f32[9,1,64,128]{3,2,1,0:T(8,128)S(1)} %collective-permute-done.3, f32[8,4,64,128]{3,2,1,0:T(8,128)S(1)} %fusion.89, f32[1,4,64,128]{3,2,1,0:T(8,128)S(1)} %bitcast.69), kind=kLoop, calls=%fused_computation.13 | loop fusion | flops 8339760 | bytes 3622752 | tf_op jit(solution)/shard_map/concatenate | solution.py:19
  69.8 4.7 %fusion.69 = f32[9,4,64,128]{3,2,1,0:T(8,128)S(1)} fusion(f32[9,6,66,130]{3,2,1,0:T(8,128)S(1)} %select_maximum_fusion.6, f32[9,1,64,128]{3,2,1,0:T(8,128)S(1)} %collective-permute-done.3, f32[8,4,64,128]{3,2,1,0:T(8,128)S(1)} %fusion.89, f32[1,4,64,128]{3,2,1,0:T(8,128)S(1)} %bitcast.70, f32[9,1,64,128]{3,2,1,0:T(8,128)S(1)} %collective-permute-done.2, ...), kind=kLoop, calls=%fused_computation.120 | loop fusion | flops 20643840 | bytes 24182784 | tf_op jit(solution)/shard_map/add | solution.py:75
  74.5 0.1 fusion.98
  74.6 0.6 fusion.88
  75.2 0.0 copy-start.57
  75.2 0.0 copy-start.59
  75.3 3.4 %collective-permute-start.5 = (f32[9,1,64,128]{3,2,1,0:T(8,128)S(1)}, f32[9,1,64,128]{3,2,1,0:T(8,128)S(1)}, u32[]{:S(2)}, u32[]{:S(2)}) collective-permute-start(f32[9,1,64,128]{3,2,1,0:T(8,128)S(1)} %get-tuple-element.24), channel_id=1, source_target_pairs={{0,2},{2,4},{4,6},{6,8},{8,10},{10,12},{12,14},{14,16},{16,18},{18... | collective-permute-start | bytes 884744 | tf_op jit(solution)/shard_map/ppermute | solution.py:15
  78.7 1.5 collective-permute-start.4
  80.2 0.5 compare_and_fusion.3
  80.7 0.1 fusion.105
  80.9 10.0 %collective-permute-done.5 = f32[9,1,64,128]{3,2,1,0:T(8,128)S(1)} collective-permute-done((f32[9,1,64,128]{3,2,1,0:T(8,128)S(1)}, f32[9,1,64,128]{3,2,1,0:T(8,128)S(1)}, u32[]{:S(2)}, u32[]{:S(2)}) %collective-permute-start.5) | collective-permute-done | bytes 294944 | tf_op jit(solution)/shard_map/ppermute | solution.py:15
  90.9 0.7 collective-permute-done.4
  91.6 2.7 %select_maximum_fusion.3 = f32[9,6,66,130]{3,2,1,0:T(8,128)S(1)} fusion(f32[9,1,64,128]{3,2,1,0:T(8,128)S(1)} %collective-permute-done.4, f32[9,1,64,128]{3,2,1,0:T(8,128)S(1)} %collective-permute-done.5, f32[8,4,64,128]{3,2,1,0:T(8,128)S(1)} %get-tuple-element.14, f32[1,4,64,128]{3,2,1,0:T(8,128)S(1)} %bitcast.66), kind=kLoop, calls=%fused_computation.10 | loop fusion | flops 8339760 | bytes 3622752 | tf_op jit(solution)/shard_map/concatenate | solution.py:19
  94.4 4.7 %fusion.44 = f32[9,4,64,128]{3,2,1,0:T(8,128)S(1)} fusion(f32[9,6,66,130]{3,2,1,0:T(8,128)S(1)} %select_maximum_fusion.3, f32[9,1,64,128]{3,2,1,0:T(8,128)S(1)} %collective-permute-done.5, f32[8,4,64,128]{3,2,1,0:T(8,128)S(1)} %get-tuple-element.14, f32[1,4,64,128]{3,2,1,0:T(8,128)S(1)} %bitcast.67, f32[9,1,64,128]{3,2,1,0:T(8,128)S(1)} %collective-permute-done.4, ...), kind=kLoop, calls=%fused_computation.87 | loop fusion | flops 20643840 | bytes 24182784 | tf_op jit(solution)/shard_map/add | solution.py:75
  99.1 0.1 fusion.97
  99.2 0.6 fusion.87
  99.8 0.9 fusion.91
  100.7 4.4 %collective-permute-start.7 = (f32[9,1,64,128]{3,2,1,0:T(8,128)}, f32[9,1,64,128]{3,2,1,0:T(8,128)}, u32[]{:S(2)}, u32[]{:S(2)}) collective-permute-start(f32[9,1,64,128]{3,2,1,0:T(8,128)} %get-tuple-element.22), channel_id=1, source_target_pairs={{0,2},{2,4},{4,6},{6,8},{8,10},{10,12},{12,14},{14,16},{16,18},{18... | collective-permute-start | bytes 884744 | tf_op jit(solution)/shard_map/ppermute | solution.py:15
  105.0 1.3 collective-permute-start.6
  106.3 0.5 compare_and_fusion.2
  106.8 8.7 %copy.10 = f32[8,4,64,128]{0,3,2,1:T(8,128)} copy(f32[8,4,64,128]{3,2,1,0:T(8,128)S(1)} %get-tuple-element.15) | data formatting | bytes 2097152 | tf_op jit(solution)/shard_map/add | solution.py:120
  115.6 7.0 %gather_fusion = f32[128,8]{1,0:T(8,128)} fusion(f32[8,32768]{0,1:T(8,128)} %bitcast.59, s32[1024]{0:T(1024)S(1)} %pad_clamp_fusion), kind=kCustom, calls=%fused_computation.clone | custom fusion | bytes 8704 | tf_op jit(solution)/shard_map/jit(_take)/gather | solution.py:121
  122.6 8.7 %copy.11 = f32[8,4,64,128]{0,3,2,1:T(8,128)} copy(f32[8,4,64,128]{3,2,1,0:T(8,128)S(1)} %get-tuple-element.13) | data formatting | bytes 2097152 | tf_op jit(solution)/shard_map/add | solution.py:120
  131.3 7.0 %gather_fusion.1 = f32[128,8]{1,0:T(8,128)} fusion(f32[8,32768]{0,1:T(8,128)} %bitcast.61, s32[1024]{0:T(1024)S(1)} %pad_clamp_fusion), kind=kCustom, calls=%fused_computation.1.clone | custom fusion | bytes 8704 | tf_op jit(solution)/shard_map/jit(_take)/gather | solution.py:121
  138.5 3.9 %select_maximum_fusion = f32[9,6,66,130]{3,2,1,0:T(8,128)S(1)} fusion(f32[9,1,64,128]{3,2,1,0:T(8,128)} %collective-permute-done.6, f32[9,1,64,128]{3,2,1,0:T(8,128)} %collective-permute-done.7, f32[8,4,64,128]{3,2,1,0:T(8,128)S(1)} %get-tuple-element.12, f32[1,4,64,128]{3,2,1,0:T(8,128)S(1)} %bitcast.63), kind=kLoop, calls=%fused_computation.7 | loop fusion | flops 8339760 | bytes 3622752 | tf_op jit(solution)/shard_map/concatenate | solution.py:19
  142.6 5.7 %fusion.19 = f32[9,4,64,128]{3,2,1,0:T(8,128)S(1)} fusion(f32[9,6,66,130]{3,2,1,0:T(8,128)S(1)} %select_maximum_fusion, f32[9,1,64,128]{3,2,1,0:T(8,128)} %collective-permute-done.7, f32[8,4,64,128]{3,2,1,0:T(8,128)S(1)} %get-tuple-element.12, f32[1,4,64,128]{3,2,1,0:T(8,128)S(1)} %bitcast.64, f32[9,1,64,128]{3,2,1,0:T(8,128)} %collective-permute-done.6, ...), kind=kLoop, calls=%fused_computation.54 | loop fusion | flops 20643840 | bytes 24182784 | tf_op jit(solution)/shard_map/add | solution.py:75
  148.3 0.1 fusion.96
  148.4 0.4 fusion.84
  148.8 0.0 copy-start
  148.8 0.0 copy-start.54
  148.9 8.8 %copy.12 = f32[8,4,64,128]{0,3,2,1:T(8,128)} copy(f32[8,4,64,128]{3,2,1,0:T(8,128)S(1)} %fusion.84) | data formatting | bytes 2097152 | tf_op jit(solution)/shard_map/add | solution.py:120
  157.6 6.4 %gather_fusion.2 = f32[128,8]{1,0:T(8,128)S(1)} fusion(f32[8,32768]{0,1:T(8,128)} %bitcast.60, s32[1024]{0:T(1024)S(1)} %pad_clamp_fusion), kind=kCustom, calls=%fused_computation.2.clone | custom fusion | bytes 8704 | tf_op jit(solution)/shard_map/jit(_take)/gather | solution.py:121
  164.1 0.1 fusion.108
  164.2 2.7 %collective-permute-start.8 = (f32[8,128]{0,1:T(8,128)S(1)}, f32[8,128]{0,1:T(8,128)S(1)}, u32[]{:S(2)}, u32[]{:S(2)}) collective-permute-start(f32[8,128]{0,1:T(8,128)S(1)} %fusion.108), channel_id=1, source_target_pairs={{0,2},{2,0},{4,6},{6,4},{8,10},{10,8},{12,14},{14,12},{16,18},{18,... | collective-permute-start | bytes 12296 | tf_op jit(solution)/shard_map/ppermute | solution.py:126
  167.0 2.2 %collective-permute-done.8 = f32[8,128]{0,1:T(8,128)S(1)} collective-permute-done((f32[8,128]{0,1:T(8,128)S(1)}, f32[8,128]{0,1:T(8,128)S(1)}, u32[]{:S(2)}, u32[]{:S(2)}) %collective-permute-start.8) | collective-permute-done | bytes 4128 | tf_op jit(solution)/shard_map/ppermute | solution.py:126
  169.2 1.7 collective-permute-start.9
  170.9 2.6 %collective-permute-done.9 = f32[8,128]{0,1:T(8,128)S(1)} collective-permute-done((f32[8,128]{0,1:T(8,128)S(1)}, f32[8,128]{0,1:T(8,128)S(1)}, u32[]{:S(2)}, u32[]{:S(2)}) %collective-permute-start.9) | collective-permute-done | bytes 4128 | tf_op jit(solution)/shard_map/ppermute | solution.py:126
  173.6 4.6 %collective-permute-start.10 = (f32[8,128]{0,1:T(8,128)S(1)}, f32[8,128]{0,1:T(8,128)S(1)}, u32[]{:S(2)}, u32[]{:S(2)}) collective-permute-start(f32[8,128]{0,1:T(8,128)S(1)} %add.337), channel_id=1, source_target_pairs={{0,8},{2,10},{4,12},{6,14},{8,0},{10,2},{12,4},{14,6},{16,24},{18,... | collective-permute-start | bytes 12296 | tf_op jit(solution)/shard_map/ppermute | solution.py:126
  178.2 2.9 %collective-permute-done.10 = f32[8,128]{0,1:T(8,128)S(1)} collective-permute-done((f32[8,128]{0,1:T(8,128)S(1)}, f32[8,128]{0,1:T(8,128)S(1)}, u32[]{:S(2)}, u32[]{:S(2)}) %collective-permute-start.10) | collective-permute-done | bytes 4128 | tf_op jit(solution)/shard_map/ppermute | solution.py:126
  181.1 2.3 %collective-permute-start.11 = (f32[8,128]{0,1:T(8,128)S(1)}, f32[8,128]{0,1:T(8,128)S(1)}, u32[]{:S(2)}, u32[]{:S(2)}) collective-permute-start(f32[8,128]{0,1:T(8,128)S(1)} %add.338), channel_id=1, source_target_pairs={{0,16},{2,18},{4,20},{6,22},{8,24},{10,26},{12,28},{14,30},{16,0},... | collective-permute-start | bytes 12296 | tf_op jit(solution)/shard_map/ppermute | solution.py:126
  183.4 2.9 %collective-permute-done.11 = f32[8,128]{0,1:T(8,128)S(1)} collective-permute-done((f32[8,128]{0,1:T(8,128)S(1)}, f32[8,128]{0,1:T(8,128)S(1)}, u32[]{:S(2)}, u32[]{:S(2)}) %collective-permute-start.11) | collective-permute-done | bytes 4128 | tf_op jit(solution)/shard_map/ppermute | solution.py:126
  186.4 0.7 copy.13
  (131 shorter events, 0.4 us)
Async XLA Ops:
  7.2 9.0 %copy-start.53 = (s32[3]{0:T(128)S(1)}, s32[3]{0:T(128)}, u32[]{:S(2)}) copy-start(s32[3]{0:T(128)} %param.13) | copy-start | bytes 40
  7.2 17.4 %copy-start.50 = (f32[4,4,64,128]{3,2,1,0:T(8,128)S(1)}, f32[4,4,64,128]{3,2,1,0:T(8,128)}, u32[]{:S(2)}) copy-start(f32[4,4,64,128]{3,2,1,0:T(8,128)} %param.11) | copy-start | bytes 1572868
  7.2 39.3 %all-reduce.7.cloned.1.call-start = ((), (), s32[]{:S(2)}) async-start(), calls=%async_computation | async-start | bytes 786432 | tf_op jit(solution)/shard_map/psum | solution.py:25
  10.0 15.4 %copy-start.58 = (f32[8,3]{0,1:T(4,128)S(1)}, f32[8,3]{0,1:T(4,128)}, u32[]{:S(2)}) copy-start(f32[8,3]{0,1:T(4,128)} %param.15) | copy-start | bytes 292
  10.0 15.4 %copy-start.60 = (s32[8]{0:T(128)S(1)}, s32[8]{0:T(128)}, u32[]{:S(2)}) copy-start(s32[8]{0:T(128)} %param.14) | copy-start | bytes 100
  10.1 15.4 %collective-permute-start = (f32[6,1,64,128]{3,2,1,0:T(8,128)S(1)}, f32[6,1,64,128]{3,2,1,0:T(8,128)S(1)}, u32[]{:S(2)}, u32[]{:S(2)}) collective-permute-start(f32[6,1,64,128]{3,2,1,0:T(8,128)S(1)} %get-tuple-element.28), channel_id=1, source_target_pairs={{0,2},{2,4},{4,6},{6,8},{8,10},{10,12},{12,14},{14,16},{16,18},{18... | collective-permute-start | bytes 589832 | tf_op jit(solution)/shard_map/ppermute | solution.py:15
  14.8 10.6 %collective-permute-start.1 = (f32[6,1,64,128]{3,2,1,0:T(8,128)S(1)}, f32[6,1,64,128]{3,2,1,0:T(8,128)S(1)}, u32[]{:S(2)}, u32[]{:S(2)}) collective-permute-start(f32[6,1,64,128]{3,2,1,0:T(8,128)S(1)} %get-tuple-element.29), channel_id=1, source_target_pairs={{2,0},{4,2},{6,4},{8,6},{10,8},{12,10},{14,12},{16,14},{18,16},{20... | collective-permute-start | bytes 589832 | tf_op jit(solution)/shard_map/ppermute | solution.py:18
  28.4 41.3 %copy-start.33 = (f32[4,64,128]{2,1,0:T(8,128)}, f32[4,64,128]{2,1,0:T(8,128)S(1)}, u32[]{:S(2)}) copy-start(f32[4,64,128]{2,1,0:T(8,128)S(1)} %get-tuple-element.39) | copy-start | bytes 393220
  28.4 41.4 %copy-start.36 = (f32[4,64,128]{2,1,0:T(8,128)}, f32[4,64,128]{2,1,0:T(8,128)S(1)}, u32[]{:S(2)}) copy-start(f32[4,64,128]{2,1,0:T(8,128)S(1)} %get-tuple-element.40) | copy-start | bytes 393220
  28.4 41.4 %copy-start.39 = (f32[4,64,128]{2,1,0:T(8,128)}, f32[4,64,128]{2,1,0:T(8,128)S(1)}, u32[]{:S(2)}) copy-start(f32[4,64,128]{2,1,0:T(8,128)S(1)} %get-tuple-element.41) | copy-start | bytes 393220
  28.4 19.1 %copy-start.1 = (f32[8,4,64,128]{3,2,1,0:T(8,128)S(1)}, f32[8,4,64,128]{3,2,1,0:T(8,128)}, u32[]{:S(2)}) copy-start(f32[8,4,64,128]{3,2,1,0:T(8,128)} %param.10) | copy-start | bytes 3145732
  28.7 41.1 %copy-start.7 = (f32[4,64,128]{2,1,0:T(8,128)}, f32[4,64,128]{2,1,0:T(8,128)S(1)}, u32[]{:S(2)}) copy-start(f32[4,64,128]{2,1,0:T(8,128)S(1)} %get-tuple-element.49) | copy-start | bytes 393220
  28.7 41.1 %copy-start.10 = (f32[4,64,128]{2,1,0:T(8,128)}, f32[4,64,128]{2,1,0:T(8,128)S(1)}, u32[]{:S(2)}) copy-start(f32[4,64,128]{2,1,0:T(8,128)S(1)} %get-tuple-element.50) | copy-start | bytes 393220
  28.7 41.1 %copy-start.13 = (f32[4,64,128]{2,1,0:T(8,128)}, f32[4,64,128]{2,1,0:T(8,128)S(1)}, u32[]{:S(2)}) copy-start(f32[4,64,128]{2,1,0:T(8,128)S(1)} %get-tuple-element.61) | copy-start | bytes 393220
  28.7 41.1 %copy-start.16 = (f32[4,64,128]{2,1,0:T(8,128)}, f32[4,64,128]{2,1,0:T(8,128)S(1)}, u32[]{:S(2)}) copy-start(f32[4,64,128]{2,1,0:T(8,128)S(1)} %get-tuple-element.62) | copy-start | bytes 393220
  28.7 41.1 %copy-start.19 = (f32[4,64,128]{2,1,0:T(8,128)}, f32[4,64,128]{2,1,0:T(8,128)S(1)}, u32[]{:S(2)}) copy-start(f32[4,64,128]{2,1,0:T(8,128)S(1)} %get-tuple-element.63) | copy-start | bytes 393220
  28.7 41.1 %copy-start.22 = (f32[4,64,128]{2,1,0:T(8,128)}, f32[4,64,128]{2,1,0:T(8,128)S(1)}, u32[]{:S(2)}) copy-start(f32[4,64,128]{2,1,0:T(8,128)S(1)} %get-tuple-element.64) | copy-start | bytes 393220
  28.7 65.6 %copy-start.5 = (f32[4,64,128]{2,1,0:T(8,128)}, f32[4,64,128]{2,1,0:T(8,128)S(1)}, u32[]{:S(2)}) copy-start(f32[4,64,128]{2,1,0:T(8,128)S(1)} %get-tuple-element.48) | copy-start | bytes 393220
  47.7 5.7 %copy-start.48 = (f32[6,66,130]{2,1,0:T(8,128)S(1)}, f32[6,66,130]{2,1,0:T(8,128)}, u32[]{:S(2)}) copy-start(f32[6,66,130]{2,1,0:T(8,128)} %get-tuple-element.16) | copy-start | bytes 617764
  47.8 5.7 %copy-start.49 = (f32[6,66,130]{2,1,0:T(8,128)S(1)}, f32[6,66,130]{2,1,0:T(8,128)}, u32[]{:S(2)}) copy-start(f32[6,66,130]{2,1,0:T(8,128)} %get-tuple-element.20) | copy-start | bytes 617764
  48.4 5.4 %copy-start.3 = (f32[4,64,128]{2,1,0:T(8,128)S(1)}, f32[4,64,128]{2,1,0:T(8,128)}, u32[]{:S(2)}) copy-start(f32[4,64,128]{2,1,0:T(8,128)} %get-tuple-element.6) | copy-start | bytes 393220
  48.4 16.7 %collective-permute-start.3 = (f32[9,1,64,128]{3,2,1,0:T(8,128)S(1)}, f32[9,1,64,128]{3,2,1,0:T(8,128)S(1)}, u32[]{:S(2)}, u32[]{:S(2)}) collective-permute-start(f32[9,1,64,128]{3,2,1,0:T(8,128)S(1)} %get-tuple-element.26), channel_id=1, source_target_pairs={{0,2},{2,4},{4,6},{6,8},{8,10},{10,12},{12,14},{14,16},{16,18},{18... | collective-permute-start | bytes 884744 | tf_op jit(solution)/shard_map/ppermute | solution.py:15
  52.1 14.9 %collective-permute-start.2 = (f32[9,1,64,128]{3,2,1,0:T(8,128)S(1)}, f32[9,1,64,128]{3,2,1,0:T(8,128)S(1)}, u32[]{:S(2)}, u32[]{:S(2)}) collective-permute-start(f32[9,1,64,128]{3,2,1,0:T(8,128)S(1)} %get-tuple-element.27), channel_id=1, source_target_pairs={{2,0},{4,2},{6,4},{8,6},{10,8},{12,10},{14,12},{16,14},{18,16},{20... | collective-permute-start | bytes 884744 | tf_op jit(solution)/shard_map/ppermute | solution.py:18
  53.7 40.6 %copy-start.25 = (f32[4,64,128]{2,1,0:T(8,128)}, f32[4,64,128]{2,1,0:T(8,128)S(1)}, u32[]{:S(2)}) copy-start(f32[4,64,128]{2,1,0:T(8,128)S(1)} %get-tuple-element.35) | copy-start | bytes 393220
  53.7 40.6 %copy-start.27 = (f32[4,64,128]{2,1,0:T(8,128)}, f32[4,64,128]{2,1,0:T(8,128)S(1)}, u32[]{:S(2)}) copy-start(f32[4,64,128]{2,1,0:T(8,128)S(1)} %get-tuple-element.36) | copy-start | bytes 393220
  53.7 40.6 %copy-start.29 = (f32[4,64,128]{2,1,0:T(8,128)}, f32[4,64,128]{2,1,0:T(8,128)S(1)}, u32[]{:S(2)}) copy-start(f32[4,64,128]{2,1,0:T(8,128)S(1)} %get-tuple-element.67) | copy-start | bytes 393220
  53.7 40.6 %copy-start.31 = (f32[4,64,128]{2,1,0:T(8,128)}, f32[4,64,128]{2,1,0:T(8,128)S(1)}, u32[]{:S(2)}) copy-start(f32[4,64,128]{2,1,0:T(8,128)S(1)} %get-tuple-element.68) | copy-start | bytes 393220
  53.8 16.0 %copy-start.42 = (f32[4,64,128]{2,1,0:T(8,128)S(1)}, f32[4,64,128]{2,1,0:T(8,128)}, u32[]{:S(2)}) copy-start(f32[4,64,128]{2,1,0:T(8,128)} %get-tuple-element.42) | copy-start | bytes 393220
  53.8 16.0 %copy-start.44 = (f32[4,64,128]{2,1,0:T(8,128)S(1)}, f32[4,64,128]{2,1,0:T(8,128)}, u32[]{:S(2)}) copy-start(f32[4,64,128]{2,1,0:T(8,128)} %get-tuple-element.65) | copy-start | bytes 393220
  53.9 16.0 %copy-start.46 = (f32[4,64,128]{2,1,0:T(8,128)S(1)}, f32[4,64,128]{2,1,0:T(8,128)}, u32[]{:S(2)}) copy-start(f32[4,64,128]{2,1,0:T(8,128)} %get-tuple-element.66) | copy-start | bytes 393220
  75.2 5.0 %copy-start.57 = (s32[128]{0:T(128)S(1)}, s32[128]{0:T(128)}, u32[]{:S(2)}) copy-start(s32[128]{0:T(128)} %param.17) | copy-start | bytes 1540
  75.2 5.0 %copy-start.59 = (s32[128]{0:T(128)S(1)}, s32[128]{0:T(128)}, u32[]{:S(2)}) copy-start(s32[128]{0:T(128)} %param.16) | copy-start | bytes 1540
  75.2 5.5 %copy-start.2 = (f32[4,64,128]{2,1,0:T(8,128)S(1)}, f32[4,64,128]{2,1,0:T(8,128)}, u32[]{:S(2)}) copy-start(f32[4,64,128]{2,1,0:T(8,128)} %get-tuple-element.7) | copy-start | bytes 393220
  75.3 15.6 %collective-permute-start.5 = (f32[9,1,64,128]{3,2,1,0:T(8,128)S(1)}, f32[9,1,64,128]{3,2,1,0:T(8,128)S(1)}, u32[]{:S(2)}, u32[]{:S(2)}) collective-permute-start(f32[9,1,64,128]{3,2,1,0:T(8,128)S(1)} %get-tuple-element.24), channel_id=1, source_target_pairs={{0,2},{2,4},{4,6},{6,8},{8,10},{10,12},{12,14},{14,16},{16,18},{18... | collective-permute-start | bytes 884744 | tf_op jit(solution)/shard_map/ppermute | solution.py:15
  78.7 12.9 %collective-permute-start.4 = (f32[9,1,64,128]{3,2,1,0:T(8,128)S(1)}, f32[9,1,64,128]{3,2,1,0:T(8,128)S(1)}, u32[]{:S(2)}, u32[]{:S(2)}) collective-permute-start(f32[9,1,64,128]{3,2,1,0:T(8,128)S(1)} %get-tuple-element.25), channel_id=1, source_target_pairs={{2,0},{4,2},{6,4},{8,6},{10,8},{12,10},{14,12},{16,14},{18,16},{20... | collective-permute-start | bytes 884744 | tf_op jit(solution)/shard_map/ppermute | solution.py:18
  80.8 13.6 %copy-start.8 = (f32[4,64,128]{2,1,0:T(8,128)S(1)}, f32[4,64,128]{2,1,0:T(8,128)}, u32[]{:S(2)}) copy-start(f32[4,64,128]{2,1,0:T(8,128)} %copy-done.7) | copy-start | bytes 393220
  80.8 13.6 %copy-start.11 = (f32[4,64,128]{2,1,0:T(8,128)S(1)}, f32[4,64,128]{2,1,0:T(8,128)}, u32[]{:S(2)}) copy-start(f32[4,64,128]{2,1,0:T(8,128)} %copy-done.10) | copy-start | bytes 393220
  80.8 13.6 %copy-start.14 = (f32[4,64,128]{2,1,0:T(8,128)S(1)}, f32[4,64,128]{2,1,0:T(8,128)}, u32[]{:S(2)}) copy-start(f32[4,64,128]{2,1,0:T(8,128)} %copy-done.13) | copy-start | bytes 393220
  80.8 13.6 %copy-start.17 = (f32[4,64,128]{2,1,0:T(8,128)S(1)}, f32[4,64,128]{2,1,0:T(8,128)}, u32[]{:S(2)}) copy-start(f32[4,64,128]{2,1,0:T(8,128)} %copy-done.16) | copy-start | bytes 393220
  80.8 13.6 %copy-start.20 = (f32[4,64,128]{2,1,0:T(8,128)S(1)}, f32[4,64,128]{2,1,0:T(8,128)}, u32[]{:S(2)}) copy-start(f32[4,64,128]{2,1,0:T(8,128)} %copy-done.19) | copy-start | bytes 393220
  80.8 13.6 %copy-start.23 = (f32[4,64,128]{2,1,0:T(8,128)S(1)}, f32[4,64,128]{2,1,0:T(8,128)}, u32[]{:S(2)}) copy-start(f32[4,64,128]{2,1,0:T(8,128)} %copy-done.22) | copy-start | bytes 393220
  80.8 13.6 %copy-start.34 = (f32[4,64,128]{2,1,0:T(8,128)S(1)}, f32[4,64,128]{2,1,0:T(8,128)}, u32[]{:S(2)}) copy-start(f32[4,64,128]{2,1,0:T(8,128)} %copy-done.33) | copy-start | bytes 393220
  80.8 13.6 %copy-start.37 = (f32[4,64,128]{2,1,0:T(8,128)S(1)}, f32[4,64,128]{2,1,0:T(8,128)}, u32[]{:S(2)}) copy-start(f32[4,64,128]{2,1,0:T(8,128)} %copy-done.36) | copy-start | bytes 393220
  80.8 13.6 %copy-start.40 = (f32[4,64,128]{2,1,0:T(8,128)S(1)}, f32[4,64,128]{2,1,0:T(8,128)}, u32[]{:S(2)}) copy-start(f32[4,64,128]{2,1,0:T(8,128)} %copy-done.39) | copy-start | bytes 393220
  100.7 37.8 %collective-permute-start.7 = (f32[9,1,64,128]{3,2,1,0:T(8,128)}, f32[9,1,64,128]{3,2,1,0:T(8,128)}, u32[]{:S(2)}, u32[]{:S(2)}) collective-permute-start(f32[9,1,64,128]{3,2,1,0:T(8,128)} %get-tuple-element.22), channel_id=1, source_target_pairs={{0,2},{2,4},{4,6},{6,8},{8,10},{10,12},{12,14},{14,16},{16,18},{18... | collective-permute-start | bytes 884744 | tf_op jit(solution)/shard_map/ppermute | solution.py:15
  105.0 33.4 %collective-permute-start.6 = (f32[9,1,64,128]{3,2,1,0:T(8,128)}, f32[9,1,64,128]{3,2,1,0:T(8,128)}, u32[]{:S(2)}, u32[]{:S(2)}) collective-permute-start(f32[9,1,64,128]{3,2,1,0:T(8,128)} %get-tuple-element.23), channel_id=1, source_target_pairs={{2,0},{4,2},{6,4},{8,6},{10,8},{12,10},{14,12},{16,14},{18,16},{20... | collective-permute-start | bytes 884744 | tf_op jit(solution)/shard_map/ppermute | solution.py:18
  138.3 4.1 %copy-start.18 = (f32[4,64,128]{2,1,0:T(8,128)S(1)}, f32[4,64,128]{2,1,0:T(8,128)}, u32[]{:S(2)}) copy-start(f32[4,64,128]{2,1,0:T(8,128)} %copy-done.16) | copy-start | bytes 393220
  138.3 4.1 %copy-start.21 = (f32[4,64,128]{2,1,0:T(8,128)S(1)}, f32[4,64,128]{2,1,0:T(8,128)}, u32[]{:S(2)}) copy-start(f32[4,64,128]{2,1,0:T(8,128)} %copy-done.19) | copy-start | bytes 393220
  138.4 4.1 %copy-start.24 = (f32[4,64,128]{2,1,0:T(8,128)S(1)}, f32[4,64,128]{2,1,0:T(8,128)}, u32[]{:S(2)}) copy-start(f32[4,64,128]{2,1,0:T(8,128)} %copy-done.22) | copy-start | bytes 393220
  138.4 4.1 %copy-start.26 = (f32[4,64,128]{2,1,0:T(8,128)S(1)}, f32[4,64,128]{2,1,0:T(8,128)}, u32[]{:S(2)}) copy-start(f32[4,64,128]{2,1,0:T(8,128)} %copy-done.25) | copy-start | bytes 393220
  138.4 4.1 %copy-start.28 = (f32[4,64,128]{2,1,0:T(8,128)S(1)}, f32[4,64,128]{2,1,0:T(8,128)}, u32[]{:S(2)}) copy-start(f32[4,64,128]{2,1,0:T(8,128)} %copy-done.27) | copy-start | bytes 393220
  138.4 4.1 %copy-start.30 = (f32[4,64,128]{2,1,0:T(8,128)S(1)}, f32[4,64,128]{2,1,0:T(8,128)}, u32[]{:S(2)}) copy-start(f32[4,64,128]{2,1,0:T(8,128)} %copy-done.29) | copy-start | bytes 393220
  138.4 4.1 %copy-start.32 = (f32[4,64,128]{2,1,0:T(8,128)S(1)}, f32[4,64,128]{2,1,0:T(8,128)}, u32[]{:S(2)}) copy-start(f32[4,64,128]{2,1,0:T(8,128)} %copy-done.31) | copy-start | bytes 393220
  138.4 4.1 %copy-start.35 = (f32[4,64,128]{2,1,0:T(8,128)S(1)}, f32[4,64,128]{2,1,0:T(8,128)}, u32[]{:S(2)}) copy-start(f32[4,64,128]{2,1,0:T(8,128)} %copy-done.33) | copy-start | bytes 393220
  148.8 8.8 %copy-start = (f32[8,4,64,128]{3,2,1,0:T(8,128)}, f32[8,4,64,128]{3,2,1,0:T(8,128)S(1)}, u32[]{:S(2)}) copy-start(f32[8,4,64,128]{3,2,1,0:T(8,128)S(1)} %fusion.84) | copy-start | bytes 3145732
  148.8 15.3 %copy-start.51 = (f32[128,8]{1,0:T(8,128)S(1)}, f32[128,8]{1,0:T(8,128)}, u32[]{:S(2)}) copy-start(f32[128,8]{1,0:T(8,128)} %gather_fusion) | copy-start | bytes 12292
  148.8 15.2 %copy-start.52 = (f32[128,8]{1,0:T(8,128)S(1)}, f32[128,8]{1,0:T(8,128)}, u32[]{:S(2)}) copy-start(f32[128,8]{1,0:T(8,128)} %gather_fusion.1) | copy-start | bytes 12292
  148.8 15.2 %copy-start.54 = (pred[128]{0:T(512)(128)(4,1)S(1)}, pred[128]{0:T(512)(128)(4,1)}, u32[]{:S(2)}) copy-start(pred[128]{0:T(512)(128)(4,1)} %get-tuple-element.8) | copy-start | bytes 388
  148.8 15.2 %copy-start.55 = (pred[128]{0:T(512)(128)(4,1)S(1)}, pred[128]{0:T(512)(128)(4,1)}, u32[]{:S(2)}) copy-start(pred[128]{0:T(512)(128)(4,1)} %get-tuple-element.56) | copy-start | bytes 388
  148.8 15.2 %copy-start.56 = (pred[128]{0:T(512)(128)(4,1)S(1)}, pred[128]{0:T(512)(128)(4,1)}, u32[]{:S(2)}) copy-start(pred[128]{0:T(512)(128)(4,1)} %get-tuple-element.55) | copy-start | bytes 388
  164.2 5.0 %collective-permute-start.8 = (f32[8,128]{0,1:T(8,128)S(1)}, f32[8,128]{0,1:T(8,128)S(1)}, u32[]{:S(2)}, u32[]{:S(2)}) collective-permute-start(f32[8,128]{0,1:T(8,128)S(1)} %fusion.108), channel_id=1, source_target_pairs={{0,2},{2,0},{4,6},{6,4},{8,10},{10,8},{12,14},{14,12},{16,18},{18,... | collective-permute-start | bytes 12296 | tf_op jit(solution)/shard_map/ppermute | solution.py:126
  169.2 4.3 %collective-permute-start.9 = (f32[8,128]{0,1:T(8,128)S(1)}, f32[8,128]{0,1:T(8,128)S(1)}, u32[]{:S(2)}, u32[]{:S(2)}) collective-permute-start(f32[8,128]{0,1:T(8,128)S(1)} %add.336), channel_id=1, source_target_pairs={{0,4},{2,6},{4,0},{6,2},{8,12},{10,14},{12,8},{14,10},{16,20},{18,... | collective-permute-start | bytes 12296 | tf_op jit(solution)/shard_map/ppermute | solution.py:126
  173.6 7.6 %collective-permute-start.10 = (f32[8,128]{0,1:T(8,128)S(1)}, f32[8,128]{0,1:T(8,128)S(1)}, u32[]{:S(2)}, u32[]{:S(2)}) collective-permute-start(f32[8,128]{0,1:T(8,128)S(1)} %add.337), channel_id=1, source_target_pairs={{0,8},{2,10},{4,12},{6,14},{8,0},{10,2},{12,4},{14,6},{16,24},{18,... | collective-permute-start | bytes 12296 | tf_op jit(solution)/shard_map/ppermute | solution.py:126
  181.1 5.2 %collective-permute-start.11 = (f32[8,128]{0,1:T(8,128)S(1)}, f32[8,128]{0,1:T(8,128)S(1)}, u32[]{:S(2)}, u32[]{:S(2)}) collective-permute-start(f32[8,128]{0,1:T(8,128)S(1)} %add.338), channel_id=1, source_target_pairs={{0,16},{2,18},{4,20},{6,22},{8,24},{10,26},{12,28},{14,30},{16,0},... | collective-permute-start | bytes 12296 | tf_op jit(solution)/shard_map/ppermute | solution.py:126
  (10 other events, 37.8 us)
Sparse Core Ops, SparseCore 0:
  25.5 20.9 all-reduce.6
